TPU v7x, 32 devices: a whole 2x2x4 slice. The times are simulated.
32 devices in a mesh: frames: 4 (over y, core), space: 8 (over z, x).
Axes of the slice: x: 2, y: 2, z: 4, core: 2. Of those that a mesh axis runs over, the one named last changes fastest.
Arguments:
- latent: bfloat16 [4, 16, 256, 1152], P('frames', 'space'), may hold values from -6 to 6
- query_rows: bfloat16 [4, 16, 256, 1152], P('frames', 'space'), may hold values from -5.5 to 5.5
- key_rows: bfloat16 [4, 16, 256, 1152], P('frames', 'space'), may hold values from -5.5 to 5.5
- value_rows: bfloat16 [4, 16, 256, 1152], P('frames', 'space'), may hold values from -6 to 6
- cached_out: bfloat16 [4, 16, 256, 1152], P('frames', 'space'), may hold values from -4 to 4
- refreshed: int32 [4, 16], P('frames', 'space'), may hold values from 0 to 1, as said below
- band_width: int32 [16], replicated, may hold values from 1 to 3, as said below
- out_weight: bfloat16 [1152, 1152], replicated, may hold values from -0.1875 to 0.1875
- temporal_weight: bfloat16 [1152, 3456], replicated, may hold values from -0.1360803 to 0.1360803
Outputs:
- mixed: bfloat16 [4, 16, 256, 1152], P('frames', 'space')
Inputs may be any that keep to these rules, and one draw needn't show every extreme that they name: `refreshed`: 1 marks a tile that is recomputed; tiles further down a frame are recomputed more often. `band_width`: at least one head reaches 3 frames.
All inputs are finite; a program needn't handle non-finite values.
Results may differ from a plain program's by a relative error of at most 0.008.
Values may be sent and summed in bfloat16 or wider, within the bound.
A program may use at most 128 MiB of HBM per device.

v0:
```python
import math

import jax
import jax.numpy as jnp
from jax import lax
from jax.sharding import PartitionSpec as P

EDGE = 64


def shifted(block, axis, distance):
    devices = range(lax.axis_size(axis))
    route = [(i - distance, i) for i in devices if i - distance in devices]
    return lax.ppermute(block, axis, route)


def soft_rows(scores):
    top = jnp.max(scores, axis=-1, keepdims=True)
    expo = jnp.exp(scores - top)
    return expo / jnp.sum(expo, axis=-1, keepdims=True)


def attend(query_rows, key_ext, value_ext, usable, head_count):
    lead = query_rows.shape[:-2]
    tok_count, width = query_rows.shape[-2:]
    span = key_ext.shape[-2]
    head_dim = width // head_count
    scaling = 1.0 / math.sqrt(head_dim)
    query5 = query_rows.reshape(lead + (tok_count, head_count, head_dim))
    key5 = key_ext.reshape(lead + (span, head_count, head_dim))
    value5 = value_ext.reshape(lead + (span, head_count, head_dim))
    scores = (
        jnp.einsum("...qhe,...khe->...hqk", query5, key5, preferred_element_type=jnp.float32)
        * scaling
    )
    scores = jnp.where(usable[..., None, None, :], scores, -jnp.inf)
    weights = soft_rows(scores).astype(jnp.bfloat16)
    result = jnp.einsum(
        "...hqk,...khe->...qhe", weights, value5, preferred_element_type=jnp.float32
    )
    return result.astype(jnp.bfloat16).reshape(lead + (tok_count, width))


def temporal_block(block, band_width, head_count, width):
    adim, sdim, bdim, idim, pdim, _ = block.shape
    head_dim = width // head_count
    scaling = 1.0 / math.sqrt(head_dim)
    query6 = block[..., :width].reshape(adim, sdim, bdim, idim, pdim, head_count, head_dim)
    key6 = block[..., width : 2 * width].reshape(adim, sdim, bdim, idim, pdim, head_count, head_dim)
    value6 = block[..., 2 * width :].reshape(adim, sdim, bdim, idim, pdim, head_count, head_dim)
    scores = (
        jnp.einsum("asbiphe,csuiphe->siphabcu", query6, key6, preferred_element_type=jnp.float32)
        * scaling
    )
    frame_index = (
        jnp.arange(adim, dtype=jnp.int32)[:, None] * bdim
        + jnp.arange(bdim, dtype=jnp.int32)[None, :]
    )
    frame_gap = jnp.abs(frame_index[:, :, None, None] - frame_index[None, None, :, :])
    allowed = frame_gap[None] <= band_width[:, None, None, None, None]
    scores = jnp.where(allowed, scores, -jnp.inf)
    flat_scores = scores.reshape(sdim, idim, pdim, head_count, adim, bdim, adim * bdim)
    weights = soft_rows(flat_scores).astype(jnp.bfloat16)
    weights = weights.reshape(sdim, idim, pdim, head_count, adim, bdim, adim, bdim)
    result = jnp.einsum(
        "siphabcu,csuiphe->asbiphe", weights, value6, preferred_element_type=jnp.float32
    )
    return result.astype(jnp.bfloat16).reshape(adim * sdim * bdim, idim, pdim, width)


def local(
    latent,
    query_rows,
    key_rows,
    value_rows,
    cached_out,
    refreshed,
    band_width,
    out_weight,
    temporal_weight,
):
    frame_count, tile_count, tok_count, width = latent.shape
    head_count = band_width.shape[0]
    last_edges = jnp.stack([key_rows[:, -1, -EDGE:], value_rows[:, -1, -EDGE:]])
    first_edges = jnp.stack([key_rows[:, 0, :EDGE], value_rows[:, 0, :EDGE]])
    from_above = shifted(last_edges, "space", 1)
    from_below = shifted(first_edges, "space", -1)
    prev_key = jnp.concatenate([from_above[0][:, None], key_rows[:, :-1, -EDGE:]], axis=1)
    prev_value = jnp.concatenate([from_above[1][:, None], value_rows[:, :-1, -EDGE:]], axis=1)
    next_key = jnp.concatenate([key_rows[:, 1:, :EDGE], from_below[0][:, None]], axis=1)
    next_value = jnp.concatenate([value_rows[:, 1:, :EDGE], from_below[1][:, None]], axis=1)
    key_ext = jnp.concatenate([prev_key, key_rows, next_key], axis=2)
    value_ext = jnp.concatenate([prev_value, value_rows, next_value], axis=2)
    span = tok_count + 2 * EDGE
    total_tiles = tile_count * lax.axis_size("space")
    tile_index = (lax.axis_index("space") * tile_count + jnp.arange(tile_count, dtype=jnp.int32))[
        :, None
    ]
    position = jnp.arange(span, dtype=jnp.int32)[None, :]
    usable = ((position >= EDGE) | (tile_index > 0)) & (
        (position < EDGE + tok_count) | (tile_index < total_tiles - 1)
    )
    usable = usable[None]
    fresh = attend(query_rows, key_ext, value_ext, usable, head_count)
    spatial = jnp.where(refreshed[:, :, None, None] == 1, fresh, cached_out)
    projected = jnp.dot(spatial.reshape(-1, width), out_weight, preferred_element_type=jnp.float32)
    hidden = (latent.astype(jnp.float32) + projected.reshape(latent.shape)).astype(jnp.bfloat16)
    hidden32 = hidden.astype(jnp.float32)
    normed = (
        hidden32 * lax.rsqrt(jnp.mean(hidden32 * hidden32, axis=-1, keepdims=True) + 1e-06)
    ).astype(jnp.bfloat16)
    frame_groups = lax.axis_size("frames")
    space_groups = lax.axis_size("space")
    block = lax.all_to_all(normed, ("frames", "space"), split_axis=2, concat_axis=0, tiled=True)
    flat = jnp.dot(
        block.reshape(-1, width), temporal_weight, preferred_element_type=jnp.float32
    ).astype(jnp.bfloat16)
    wide_block = flat.reshape(block.shape[:-1] + (3 * width,))
    shaped = wide_block.reshape(
        frame_groups, space_groups, frame_count, wide_block.shape[1], wide_block.shape[2], 3 * width
    )
    attended = temporal_block(shaped, band_width, head_count, width)
    temporal = lax.all_to_all(
        attended, ("frames", "space"), split_axis=0, concat_axis=2, tiled=True
    )
    return (hidden32 + temporal.astype(jnp.float32)).astype(jnp.bfloat16)


def solution(mesh):
    return jax.shard_map(
        local,
        mesh=mesh,
        in_specs=(
            P("frames", "space", None, None),
            P("frames", "space", None, None),
            P("frames", "space", None, None),
            P("frames", "space", None, None),
            P("frames", "space", None, None),
            P("frames", "space"),
            P(),
            P(),
            P(),
        ),
        out_specs=P("frames", "space", None, None),
        check_vma=False,
    )
```

profile of v0, /device:TPU:0, one launch (start us, length us, event | category | flops | bytes accessed | tf_op | source)
XLA Modules:
  0.0 184.8 jit_solution(11890981346100956253)
XLA Ops:
  0.0 0.0 copy-start
  0.0 1.6 fusion.35
  1.6 0.0 copy-start.5
  1.6 5.6 %collective-permute-start = (bf16[2,1,64,1152]{3,2,1,0:T(8,128)(2,1)S(1)}, bf16[2,1,64,1152]{3,2,1,0:T(8,128)(2,1)}, u32[]{:S(2)}, u32[]{:S(2)}) collective-permute-start(bf16[2,1,64,1152]{3,2,1,0:T(8,128)(2,1)S(1)} %pad_maximum_fusion), channel_id=1, source_target_pairs={{0,1},{1,2},{2,3},{3,4},{4,5},{5,6},{6,7},{8,9},{9,10},{10,11},{11... | collective-permute-start | bytes 884744 | tf_op jit(solution)/shard_map/ppermute | solution.py:14
  7.2 0.7 pad_maximum_fusion.1
  7.9 1.3 collective-permute-start.1
  9.3 2.4 %copy.56 = bf16[1,2,256,1152]{2,3,1,0:T(8,128)(2,1)} copy(bf16[1,2,256,1152]{3,2,1,0:T(8,128)(2,1)} %param.10) | data formatting | bytes 2359296 | tf_op args[1]
  11.7 0.1 or_and_fusion
  11.7 7.3 %collective-permute-done = bf16[2,1,64,1152]{3,2,1,0:T(8,128)(2,1)} collective-permute-done((bf16[2,1,64,1152]{3,2,1,0:T(8,128)(2,1)S(1)}, bf16[2,1,64,1152]{3,2,1,0:T(8,128)(2,1)}, u32[]{:S(2)}, u32[]{:S(2)}) %collective-permute-start) | collective-permute-done | bytes 294944 | tf_op jit(solution)/shard_map/ppermute | solution.py:14
  19.1 1.0 fusion.37
  20.1 0.0 collective-permute-done.1
  20.1 1.0 fusion.38
  21.1 2.6 %maximum_maximum_fusion.1 = bf16[1,2,384,1152]{3,2,1,0:T(8,128)(2,1)} fusion(bf16[1,1,64,1152]{3,2,1,0:T(8,128)(2,1)S(1)} %get-tuple-element.18, bf16[1,1,64,1152]{3,2,1,0:T(8,128)(2,1)S(1)} %get-tuple-element.11, bf16[1,2,256,1152]{3,2,1,0:T(8,128)(2,1)} %param.11, bf16[1,1,64,1152]{3,2,1,0:T(8,128)(2,1)S(1)} %get-tuple-element.8, ...), kind=kLoop, calls=%fused_computation.30 | loop fusion | flops 8847360 | bytes 3538944 | tf_op jit(solution)/shard_map/concatenate | solution.py:92
  23.7 3.9 %copy.55 = bf16[1,2,384,1152]{2,3,1,0:T(8,128)(2,1)} copy(bf16[1,2,384,1152]{3,2,1,0:T(8,128)(2,1)} %maximum_maximum_fusion.1) | data formatting | bytes 3538944 | tf_op jit(solution)/shard_map/concatenate | solution.py:92
  27.6 2.6 %maximum_maximum_fusion = bf16[1,2,384,1152]{3,2,1,0:T(8,128)(2,1)} fusion(bf16[1,1,64,1152]{3,2,1,0:T(8,128)(2,1)S(1)} %get-tuple-element.19, bf16[1,1,64,1152]{3,2,1,0:T(8,128)(2,1)S(1)} %get-tuple-element.26, bf16[1,2,256,1152]{3,2,1,0:T(8,128)(2,1)} %param.12, bf16[1,1,64,1152]{3,2,1,0:T(8,128)(2,1)S(1)} %get-tuple-element.25, ...), kind=kLoop, calls=%fused_computation.29 | loop fusion | flops 8847360 | bytes 3538944 | tf_op jit(solution)/shard_map/concatenate | solution.py:93
  30.2 3.9 %copy.54 = bf16[1,2,384,1152]{2,3,1,0:T(8,128)(2,1)} copy(bf16[1,2,384,1152]{3,2,1,0:T(8,128)(2,1)} %maximum_maximum_fusion) | data formatting | bytes 3538944 | tf_op jit(solution)/shard_map/concatenate | solution.py:93
  34.1 11.4 %fusion.39 = (f32[2,16,256]{2,1,0:T(8,128)S(1)}, f32[2,16,256,384]{2,3,1,0:T(8,128)}) fusion(pred[2,384]{1,0:T(4,128)(4,1)S(1)} %or_and_fusion, bf16[2,384,16,72]{1,3,2,0:T(8,128)(2,1)} %bitcast.83, bf16[2,256,16,72]{1,3,2,0:T(8,128)(2,1)} %bitcast.85), kind=kOutput, calls=%fused_computation.61 | convolution fusion | flops 465568128 | bytes 15565568 | tf_op jit(solution)/shard_map/sub | solution.py:19
  45.5 7.4 %fusion.22 = bf16[2,16,72,256]{3,2,1,0:T(8,128)(2,1)} fusion(bf16[2,384,16,72]{1,3,2,0:T(8,128)(2,1)} %bitcast.84, f32[2,16,256,384]{2,3,1,0:T(8,128)} %get-tuple-element.21, f32[2,16,256]{2,1,0:T(8,128)S(1)} %get-tuple-element.20), kind=kOutput, calls=%fused_computation.31 | convolution fusion | flops 459866112 | bytes 15564800 | tf_op jit(solution)/shard_map/...hqk,...khe->...qhe/dot_general | solution.py:38
  52.9 2.4 %copy.58 = bf16[1,2,256,1152]{3,2,1,0:T(8,128)(2,1)} copy(bf16[1,2,256,1152]{2,3,1,0:T(8,128)(2,1)} %bitcast.86) | data formatting | bytes 2359296 | tf_op jit(solution)/shard_map/reshape | solution.py:41
  55.3 0.0 copy-done
  55.3 4.0 %fusion.12 = (f32[2,256]{1,0:T(2,128)S(1)}, bf16[1,2,256,1152]{3,2,1,0:T(8,128)(2,1)S(1)}) fusion(bf16[1152,1152]{1,0:T(8,128)(2,1)S(1)} %copy-done, bf16[1,2,256,1152]{3,2,1,0:T(8,128)(2,1)} %copy.58, bf16[1,2,256,1152]{3,2,1,0:T(8,128)(2,1)} %param.13, pred[2]{0:T(512)(128)(4,1)S(1)} %compare_bitcast_fusion, bf16[1,2,256,1152]{3,2,1,0:T(8,128)(2,1)} %param.9), kind=kOutput, calls=%fused_computation.19 | convolution fusion | flops 1363082752 | bytes 7374850 | tf_op jit(solution)/shard_map/dot_general | solution.py:106
  59.3 0.0 copy-start.2
  59.3 1.0 copy-done.2
  60.3 0.3 fusion.13
  60.6 0.0 copy-start.4
  60.6 2.2 %copy.59 = bf16[1,2,256,1152]{3,1,0,2:T(2,128)(2,1)} copy(bf16[1,2,256,1152]{3,2,1,0:T(8,128)(2,1)S(1)} %fusion.13) | data formatting | bytes 2359296 | tf_op jit(solution)/shard_map/convert_element_type | solution.py:111
  62.8 6.1 %all-to-all-start = ((bf16[1,2,256,1152]{3,1,0,2:T(2,128)(2,1)}), bf16[1,2,256,1152]{3,1,0,2:T(2,128)(2,1)S(1)}, u32[]{:S(2)}, u32[]{:S(2)}) async-start(bf16[1,2,256,1152]{3,1,0,2:T(2,128)(2,1)} %copy.59), calls=%async_computation | async-start | bytes 2359296 | tf_op jit(solution)/shard_map/all_to_all | solution.py:114
  68.9 0.1 broadcast_compare_fusion
  69.0 30.1 %all-to-all-done = bf16[1,2,256,1152]{3,1,0,2:T(2,128)(2,1)S(1)} async-done(((bf16[1,2,256,1152]{3,1,0,2:T(2,128)(2,1)}), bf16[1,2,256,1152]{3,1,0,2:T(2,128)(2,1)S(1)}, u32[]{:S(2)}, u32[]{:S(2)}) %all-to-all-start) | async-done | bytes 1179680 | tf_op jit(solution)/shard_map/all_to_all | solution.py:114
  99.1 0.1 copy.80
  99.3 0.1 copy.61
  99.4 8.3 %convolution_convert_fusion = bf16[512,3456]{1,0:T(8,128)(2,1)S(1)} fusion(bf16[512,1152]{1,0:T(8,128)(2,1)S(1)} %bitcast.87, bf16[1152,3456]{1,0:T(8,128)(2,1)} %param.17), kind=kOutput, calls=%fused_computation.11 | convolution fusion | flops 4078632960 | bytes 12681216 | tf_op jit(solution)/shard_map/dot_general | solution.py:115
  107.7 1.4 fusion.34
  109.1 5.7 %reshape.245 = bf16[4,8,2,8,16,72]{5,4,3,2,1,0:T(8,128)(2,1)} reshape(bf16[4,8,1,2,8,1152]{5,4,3,1,0,2:T(8,128)(2,1)} %get-tuple-element.7) | data formatting | bytes 2359296 | tf_op jit(solution)/shard_map/reshape.30
  114.8 4.7 %reshape.246 = bf16[4,8,2,8,16,72]{5,4,3,2,1,0:T(8,128)(2,1)} reshape(bf16[4,8,1,2,8,1152]{5,4,3,1,0,2:T(8,128)(2,1)S(1)} %get-tuple-element.6) | data formatting | bytes 2359296 | tf_op jit(solution)/shard_map/reshape.31
  119.4 7.0 %fusion.17 = f32[8,2,8,16,4,4]{4,5,3,2,1,0:T(4,128)} fusion(bf16[4,8,2,8,16,72]{5,4,3,2,1,0:T(8,128)(2,1)} %reshape.246, bf16[4,8,2,8,16,72]{5,4,3,2,1,0:T(8,128)(2,1)} %reshape.245), kind=kOutput, calls=%fused_computation.25 | convolution fusion | flops 4718592 | bytes 2490368 | tf_op jit(solution)/shard_map/asbiphe,csuiphe->siphabcu/dot_general | solution.py:52
  126.4 5.4 %copy.64 = f32[8,2,8,16,4,4]{3,2,5,4,1,0:T(8,128)S(1)} copy(f32[8,2,8,16,4,4]{4,5,3,2,1,0:T(4,128)} %fusion.17) | data formatting | bytes 262144 | tf_op jit(solution)/shard_map/asbiphe,csuiphe->siphabcu/dot_general | solution.py:52
  131.9 0.2 fusion.28
  132.0 0.3 fusion.29
  132.3 0.3 divide_convert_fusion.4
  132.6 4.2 %copy.66 = bf16[8,2,8,16,4,4]{5,4,3,2,1,0:T(4,128)(2,1)} copy(bf16[8,2,8,16,4,4]{3,2,5,4,1,0:T(8,128)(2,1)S(1)} %divide_convert_fusion.4) | data formatting | bytes 131072 | tf_op jit(solution)/shard_map/convert_element_type | solution.py:63
  136.8 4.7 %reshape.244 = bf16[4,8,2,8,16,72]{5,4,3,2,1,0:T(8,128)(2,1)} reshape(bf16[4,8,1,2,8,1152]{5,4,3,1,0,2:T(8,128)(2,1)S(1)} %get-tuple-element.5) | data formatting | bytes 2359296 | tf_op jit(solution)/shard_map/reshape.35
  141.5 4.5 %convert_bitcast_fusion.1 = bf16[4,8,1,2,8,16,72]{6,0,5,4,3,1,2:T(4,128)(2,1)S(1)} fusion(bf16[8,2,8,16,4,4]{5,4,3,2,1,0:T(4,128)(2,1)} %copy.66, bf16[4,8,2,8,16,72]{5,4,3,2,1,0:T(8,128)(2,1)} %reshape.244), kind=kOutput, calls=%fused_computation.28 | convolution fusion | flops 5308416 | bytes 2424832 | tf_op jit(solution)/shard_map/siphabcu,csuiphe->asbiphe/dot_general | solution.py:65
  146.0 0.5 copy.67
  146.5 3.4 %reshape.247 = bf16[32,2,8,1152]{3,2,1,0:T(8,128)(2,1)} reshape(bf16[4,8,1,2,8,16,72]{6,5,4,3,1,0,2:T(8,128)(2,1)S(1)} %copy.67) | data formatting | bytes 2359296 | tf_op jit(solution)/shard_map/reshape | solution.py:68
  150.0 33.6 %all_to_all.24 = bf16[32,2,8,1152]{3,2,1,0:T(8,128)(2,1)S(1)} all-to-all(bf16[32,2,8,1152]{3,2,1,0:T(8,128)(2,1)} %reshape.247), channel_id=1, replica_groups=mesh['frames'=4,'space'=8] {'frames','space'}, dimensions={0} | all-to-all | bytes 2359296 | tf_op jit(solution)/shard_map/all_to_all | solution.py:123
  183.5 0.0 copy-done.3
  183.5 1.3 fusion.14
  (11 shorter events, 0.1 us)
Async XLA Ops:
  0.0 55.3 %copy-start = (bf16[1152,1152]{1,0:T(8,128)(2,1)S(1)}, bf16[1152,1152]{1,0:T(8,128)(2,1)}, u32[]{:S(2)}) copy-start(bf16[1152,1152]{1,0:T(8,128)(2,1)} %param.16) | copy-start | bytes 7962628
  1.6 10.0 %copy-start.5 = (s32[1,2]{1,0:T(1,128)S(1)}, s32[1,2]{1,0:T(1,128)}, u32[]{:S(2)}) copy-start(s32[1,2]{1,0:T(1,128)} %param.14) | copy-start | bytes 28
  1.6 17.4 %collective-permute-start = (bf16[2,1,64,1152]{3,2,1,0:T(8,128)(2,1)S(1)}, bf16[2,1,64,1152]{3,2,1,0:T(8,128)(2,1)}, u32[]{:S(2)}, u32[]{:S(2)}) collective-permute-start(bf16[2,1,64,1152]{3,2,1,0:T(8,128)(2,1)S(1)} %pad_maximum_fusion), channel_id=1, source_target_pairs={{0,1},{1,2},{2,3},{3,4},{4,5},{5,6},{6,7},{8,9},{9,10},{10,11},{11... | collective-permute-start | bytes 884744 | tf_op jit(solution)/shard_map/ppermute | solution.py:14
  7.9 12.1 %collective-permute-start.1 = (bf16[2,1,64,1152]{3,2,1,0:T(8,128)(2,1)}, bf16[2,1,64,1152]{3,2,1,0:T(8,128)(2,1)}, u32[]{:S(2)}, u32[]{:S(2)}) collective-permute-start(bf16[2,1,64,1152]{3,2,1,0:T(8,128)(2,1)} %pad_maximum_fusion.1), channel_id=1, source_target_pairs={{1,0},{2,1},{3,2},{4,3},{5,4},{6,5},{7,6},{9,8},{10,9},{11,10},{12... | collective-permute-start | bytes 884744 | tf_op jit(solution)/shard_map/ppermute | solution.py:14
  59.3 1.0 copy-start.2
  60.6 8.4 %copy-start.4 = (s32[16]{0:T(128)S(1)}, s32[16]{0:T(128)}, u32[]{:S(2)}) copy-start(s32[16]{0:T(128)} %param.15) | copy-start | bytes 196
  62.8 36.3 %all-to-all-start = ((bf16[1,2,256,1152]{3,1,0,2:T(2,128)(2,1)}), bf16[1,2,256,1152]{3,1,0,2:T(2,128)(2,1)S(1)}, u32[]{:S(2)}, u32[]{:S(2)}) async-start(bf16[1,2,256,1152]{3,1,0,2:T(2,128)(2,1)} %copy.59), calls=%async_computation | async-start | bytes 2359296 | tf_op jit(solution)/shard_map/all_to_all | solution.py:114
  150.0 33.6 %copy-start.3 = (bf16[1,2,256,1152]{3,2,1,0:T(8,128)(2,1)S(1)}, bf16[1,2,256,1152]{3,2,1,0:T(8,128)(2,1)}, u32[]{:S(2)}) copy-start(bf16[1,2,256,1152]{3,2,1,0:T(8,128)(2,1)} %copy-done.2) | copy-start | bytes 3538948
  150.0 34.9 %copy-start.1 = (bf16[1152,1152]{1,0:T(8,128)(2,1)S(1)}, bf16[1152,1152]{1,0:T(8,128)(2,1)}, u32[]{:S(2)}) copy-start(bf16[1152,1152]{1,0:T(8,128)(2,1)} %param.16) | copy-start | bytes 7962628
where the time goes:
time: 186 us; the launch traced here: 185 us
  local copies, waits for them, and re-layouts  49.4 us (27%)
  matrix products  42.7 us (23%)
  waiting for transfers between devices  37.4 us (20%)
  blocking collectives  33.6 us (18%)
  starting transfers between devices  12.9 us (7%)
  other arithmetic  8.57 us (5%)
    all_to_all x1, blocking collectives, local(): lax.all_to_all(attended, ('frames', 'space'), split_axis=0, concat_axis=2...  33.6 us
    all_to_all x1, waiting for transfers between devices, local(): lax.all_to_all(normed, ('frames', 'space'), split_axis=2, concat_axis=0,...  30.1 us
    another operation x3, local copies, waits for them, and re-layouts  15 us
    sub x1, matrix products, soft_rows(): expo = jnp.exp(scores - top)  11.4 us
    dot_general x1, matrix products, local(): jnp.dot(block.reshape(-1, width), temporal_weight, preferred_element_type...  8.35 us
    dot_general x1, matrix products, attend(): jnp.einsum('...hqk,...khe->...qhe', weights, value5, preferred_element_ty...  7.45 us
    ppermute x2, waiting for transfers between devices, shifted(): return lax.ppermute(block, axis, route)  7.33 us
    dot_general x1, matrix products, temporal_block(): jnp.einsum('asbiphe,csuiphe->siphabcu', query6, key6, preferred_element_t...  6.99 us
  transfers between devices with their start and end apart: 3, of which 2 were waited for; matrix products, arithmetic and copies ran while one was open for 2% of the time, Pallas kernels for 0%

commit v1 on v0

v1 whole, which is shorter than its diff:
```python
import functools
import math

import jax
import jax.numpy as jnp
from jax import lax
from jax.experimental import pallas as pl
from jax.experimental.pallas import tpu as pltpu
from jax.sharding import PartitionSpec as P

EDGE = 64
LANES = 128
MESH = pl.DeviceIdType.MESH


def kernel(
    frames,
    groups,
    heads,
    latent_hbm,
    query_hbm,
    key_hbm,
    value_hbm,
    cached_hbm,
    refreshed_ref,
    band_ref,
    out_weight_hbm,
    temporal_weight_hbm,
    mixed_ref,
    query,
    key,
    value,
    latent,
    cached,
    out_weight,
    temporal_weight,
    spatial,
    hidden,
    normed,
    arrived,
    packed,
    attended,
    returned,
    gather,
    spread,
    load_sem,
    edge_send,
    edge_recv,
    norm_send,
    norm_recv,
    back_send,
    back_recv,
):
    _, tiles, rows, width = latent_hbm.shape
    share = rows // frames
    span = rows + 2 * EDGE
    head_dim = width // heads
    me = lax.axis_index("frames")
    at = lax.axis_index("space")
    has_above = at > 0
    has_below = at < groups - 1

    loads = []

    def load(src, dst):
        copy = pltpu.make_async_copy(src, dst, load_sem.at[len(loads)])
        copy.start()
        loads.append(copy)

    for t in range(tiles):
        load(query_hbm.at[0, t], query.at[t])
        for src, dst in ((key_hbm, key), (value_hbm, value)):
            load(src.at[0, t], dst.at[t, pl.ds(EDGE, rows)])
            if t > 0:
                load(src.at[0, t - 1, pl.ds(rows - EDGE, EDGE)], dst.at[t, pl.ds(0, EDGE)])
            if t < tiles - 1:
                load(src.at[0, t + 1, pl.ds(0, EDGE)], dst.at[t, pl.ds(rows + EDGE, EDGE)])
    load(cached_hbm.at[0], cached)
    load(latent_hbm.at[0], latent)
    load(out_weight_hbm, out_weight)
    early = len(loads)
    load(temporal_weight_hbm, temporal_weight)

    barrier = pltpu.get_barrier_semaphore()
    for d in range(1, frames):
        pl.semaphore_signal(
            barrier, inc=1, device_id={"frames": lax.rem(me + d, frames)}, device_id_type=MESH
        )

    @pl.when(has_above)
    def _():
        pl.semaphore_signal(barrier, inc=1, device_id={"space": at - 1}, device_id_type=MESH)

    @pl.when(has_below)
    def _():
        pl.semaphore_signal(barrier, inc=1, device_id={"space": at + 1}, device_id_type=MESH)

    peers = frames - 1 + jnp.where(has_above, 1, 0) + jnp.where(has_below, 1, 0)
    pl.semaphore_wait(barrier, peers)

    def edge(i, which, target):
        src, dst = ((key_hbm, key), (value_hbm, value))[i]
        if which == 0:
            source = src.at[0, tiles - 1, pl.ds(rows - EDGE, EDGE)]
            place = dst.at[0, pl.ds(0, EDGE)]
        else:
            source = src.at[0, 0, pl.ds(0, EDGE)]
            place = dst.at[tiles - 1, pl.ds(rows + EDGE, EDGE)]
        return pltpu.make_async_remote_copy(
            src_ref=source,
            dst_ref=place,
            send_sem=edge_send.at[which, i],
            recv_sem=edge_recv.at[which, i],
            device_id={"space": target},
            device_id_type=MESH,
        )

    @pl.when(has_below)
    def _():
        for i in range(2):
            edge(i, 0, at + 1).start()

    @pl.when(has_above)
    def _():
        for i in range(2):
            edge(i, 1, at - 1).start()

    @pl.when(jnp.logical_not(has_above))
    def _():
        for dst in (key, value):
            dst[0, pl.ds(0, EDGE)] = jnp.zeros((EDGE, width), dst.dtype)

    @pl.when(jnp.logical_not(has_below))
    def _():
        for dst in (key, value):
            dst[tiles - 1, pl.ds(rows + EDGE, EDGE)] = jnp.zeros((EDGE, width), dst.dtype)

    column = lax.broadcasted_iota(jnp.int32, (width, LANES), 0)
    first = lax.broadcasted_iota(jnp.int32, (width, LANES), 1) * head_dim
    inside = jnp.where((column >= first) & (column < first + head_dim), 1.0, 0.0)
    gather[...] = inside.astype(jnp.bfloat16)
    column = lax.broadcasted_iota(jnp.int32, (LANES, width), 1)
    first = lax.broadcasted_iota(jnp.int32, (LANES, width), 0) * head_dim
    inside = jnp.where((column >= first) & (column < first + head_dim), 1.0, 0.0)
    spread[...] = inside.astype(jnp.bfloat16)
    lane = lax.broadcasted_iota(jnp.int32, (1, LANES), 1)
    band = jnp.zeros((1, LANES), jnp.int32)
    for h in range(heads):
        band = jnp.where(lane == h, band_ref[h], band)

    for copy in loads[:early]:
        copy.wait()

    @pl.when(has_above)
    def _():
        for i in range(2):
            edge(i, 0, at - 1).wait_recv()

    @pl.when(has_below)
    def _():
        for i in range(2):
            edge(i, 1, at + 1).wait_recv()

    scale = math.log2(math.e) / math.sqrt(head_dim)
    position = lax.broadcasted_iota(jnp.int32, (1, span), 1)

    def norm_copy(t, d):
        peer = lax.rem(me + d, frames)
        return pltpu.make_async_remote_copy(
            src_ref=normed.at[t, peer],
            dst_ref=arrived.at[t, me],
            send_sem=norm_send.at[t, d],
            recv_sem=norm_recv.at[t, d],
            device_id={"frames": peer},
            device_id_type=MESH,
        )

    def back_copy(t, d):
        peer = lax.rem(me + d, frames)
        return pltpu.make_async_remote_copy(
            src_ref=attended.at[t, peer],
            dst_ref=returned.at[t, me],
            send_sem=back_send.at[t, d],
            recv_sem=back_recv.at[t, d],
            device_id={"frames": peer},
            device_id_type=MESH,
        )

    def spatial_tile(t, carry):
        whole = at * tiles + t
        low = jnp.where(whole == 0, EDGE, 0)
        high = jnp.where(whole == groups * tiles - 1, rows + EDGE, span)
        bias = jnp.where((position >= low) & (position < high), 0.0, -jnp.inf)
        fresh_here = refreshed_ref[0, t] == 1
        partial = None
        for h in range(heads):
            start, stop = h * head_dim, (h + 1) * head_dim
            a, b = start // LANES, -(-stop // LANES)
            cols = slice(a * LANES, b * LANES)
            at_col = lax.broadcasted_iota(jnp.int32, (1, (b - a) * LANES), 1) + a * LANES
            mine = (at_col >= start) & (at_col < stop)
            q = query[t, :, cols] * jnp.where(mine, 1.0, 0.0).astype(jnp.bfloat16)
            scores = lax.dot_general(
                q, key[t, :, cols], (((1,), (1,)), ((), ())), preferred_element_type=jnp.float32
            )
            scores = scores + bias
            top = jnp.max(scores, axis=-1, keepdims=True)
            expo = jnp.exp2((scores - top) * scale)
            total = jnp.sum(expo, axis=-1, keepdims=True)
            out = jnp.dot(
                expo.astype(jnp.bfloat16), value[t, :, cols], preferred_element_type=jnp.float32
            )
            out = out * (1.0 / total)
            for block in range(a, b):
                piece = out[:, (block - a) * LANES : (block - a + 1) * LANES]
                if start > block * LANES:
                    piece = jnp.where(lane + block * LANES >= start, piece, partial)
                if stop >= (block + 1) * LANES:
                    old = cached[t, :, block * LANES : (block + 1) * LANES]
                    spatial[:, block * LANES : (block + 1) * LANES] = jnp.where(
                        fresh_here, piece.astype(jnp.bfloat16), old
                    )
                else:
                    partial = piece
        projected = jnp.dot(spatial[...], out_weight[...], preferred_element_type=jnp.float32)
        hid = (latent[t].astype(jnp.float32) + projected).astype(jnp.bfloat16)
        hidden[t] = hid
        hid32 = hid.astype(jnp.float32)
        mean = jnp.mean(hid32 * hid32, axis=-1, keepdims=True)
        norm = (hid32 * lax.rsqrt(mean + 1e-06)).astype(jnp.bfloat16)
        normed[t] = norm.reshape(frames, share, width)
        for d in range(1, frames):
            norm_copy(t, frames - d).start()
        arrived[t, me] = normed[t, me]
        return carry

    lax.fori_loop(0, tiles, spatial_tile, 0)
    loads[early].wait()

    def temporal_tile(t, carry):
        for d in range(1, frames):
            norm_in(t, d)
        block = arrived[t].reshape(frames * share, width)

        def project(j, c):
            w = temporal_weight[:, pl.ds(pl.multiple_of(j * width, LANES), width)]
            flat = jnp.dot(block, w, preferred_element_type=jnp.float32).astype(jnp.bfloat16)
            packed[j] = flat.reshape(frames, share, width)
            return c

        lax.fori_loop(0, 3, project, 0)
        for d in range(1, frames + 1):
            f = lax.rem(me + frames - d, frames)
            products = packed[0, f][None] * packed[1]
            scores = jnp.dot(
                products.reshape(frames * share, width),
                gather[...],
                preferred_element_type=jnp.float32,
            ).reshape(frames, share, LANES)
            scores = [
                jnp.where(jnp.abs(f - g) <= band, scores[g], -jnp.inf) for g in range(frames)
            ]
            top = functools.reduce(jnp.maximum, scores)
            expo = [jnp.exp2((s - top) * scale) for s in scores]
            inverse = 1.0 / functools.reduce(jnp.add, expo)
            weights = jnp.stack([(e * inverse).astype(jnp.bfloat16) for e in expo])
            wide = jnp.dot(
                weights.reshape(frames * share, LANES),
                spread[...],
                preferred_element_type=jnp.float32,
            ).reshape(frames, share, width)
            result = wide[0] * packed[2, 0].astype(jnp.float32)
            for g in range(1, frames):
                result = result + wide[g] * packed[2, g].astype(jnp.float32)
            result = result.astype(jnp.bfloat16)
            if d < frames:
                attended[t, f] = result
                back_copy(t, frames - d).start()
            else:
                returned[t, me] = result
        return carry

    def norm_in(t, d):
        sender = lax.rem(me + frames - d, frames)
        pltpu.make_async_remote_copy(
            src_ref=normed.at[t, sender],
            dst_ref=arrived.at[t, sender],
            send_sem=norm_send.at[t, d],
            recv_sem=norm_recv.at[t, d],
            device_id={"frames": sender},
            device_id_type=MESH,
        ).wait_recv()

    lax.fori_loop(0, tiles, temporal_tile, 0)

    for t in range(tiles):
        for d in range(frames):
            owner = lax.rem(me + frames - d, frames)
            if d:
                pltpu.make_async_remote_copy(
                    src_ref=attended.at[t, owner],
                    dst_ref=returned.at[t, owner],
                    send_sem=back_send.at[t, d],
                    recv_sem=back_recv.at[t, d],
                    device_id={"frames": owner},
                    device_id_type=MESH,
                ).wait_recv()
            here = pl.ds(pl.multiple_of(owner * share, share), share)
            mixed_ref[0, t, here] = (
                hidden[t, here].astype(jnp.float32) + returned[t, owner].astype(jnp.float32)
            ).astype(jnp.bfloat16)

    for t in range(tiles):
        for d in range(1, frames):
            norm_copy(t, d).wait_send()
            back_copy(t, d).wait_send()

    @pl.when(has_below)
    def _():
        for i in range(2):
            edge(i, 0, at + 1).wait_send()

    @pl.when(has_above)
    def _():
        for i in range(2):
            edge(i, 1, at - 1).wait_send()


def local(
    latent,
    query_rows,
    key_rows,
    value_rows,
    cached_out,
    refreshed,
    band_width,
    out_weight,
    temporal_weight,
):
    frame_count, tiles, rows, width = latent.shape
    assert frame_count == 1
    heads = band_width.shape[0]
    frames = lax.axis_size("frames")
    groups = lax.axis_size("space")
    share = rows // frames
    span = rows + 2 * EDGE
    bf16 = latent.dtype
    anywhere = pl.BlockSpec(memory_space=pl.ANY)
    scalars = pl.BlockSpec(memory_space=pltpu.SMEM)
    dma = pltpu.SemaphoreType.DMA
    exchanged = pltpu.VMEM((tiles, frames, share, width), bf16)
    return pl.pallas_call(
        functools.partial(kernel, frames, groups, heads),
        out_shape=jax.ShapeDtypeStruct(latent.shape, bf16),
        in_specs=[anywhere] * 5 + [scalars] * 2 + [anywhere] * 2,
        out_specs=pl.BlockSpec(memory_space=pltpu.VMEM),
        scratch_shapes=[
            pltpu.VMEM((tiles, rows, width), bf16),
            pltpu.VMEM((tiles, span, width), bf16),
            pltpu.VMEM((tiles, span, width), bf16),
            pltpu.VMEM((tiles, rows, width), bf16),
            pltpu.VMEM((tiles, rows, width), bf16),
            pltpu.VMEM(out_weight.shape, bf16),
            pltpu.VMEM(temporal_weight.shape, bf16),
            pltpu.VMEM((rows, width), bf16),
            pltpu.VMEM((tiles, rows, width), bf16),
            exchanged,
            exchanged,
            pltpu.VMEM((3, frames, share, width), bf16),
            exchanged,
            exchanged,
            pltpu.VMEM((width, LANES), bf16),
            pltpu.VMEM((LANES, width), bf16),
            dma((3 * tiles + 4 * (tiles - 1) + 4,)),
            dma((2, 2)),
            dma((2, 2)),
            dma((tiles, frames)),
            dma((tiles, frames)),
            dma((tiles, frames)),
            dma((tiles, frames)),
        ],
        compiler_params=pltpu.CompilerParams(
            collective_id=0, has_side_effects=True, vmem_limit_bytes=60 * 1024 * 1024
        ),
        cost_estimate=pl.CostEstimate(
            flops=12 * 10**9, bytes_accessed=18 * 10**6, transcendentals=3 * 10**6
        ),
    )(
        latent,
        query_rows,
        key_rows,
        value_rows,
        cached_out,
        refreshed,
        band_width,
        out_weight,
        temporal_weight,
    )


def solution(mesh):
    return jax.shard_map(
        local,
        mesh=mesh,
        in_specs=(
            P("frames", "space", None, None),
            P("frames", "space", None, None),
            P("frames", "space", None, None),
            P("frames", "space", None, None),
            P("frames", "space", None, None),
            P("frames", "space"),
            P(),
            P(),
            P(),
        ),
        out_specs=P("frames", "space", None, None),
        check_vma=False,
    )
```

time: 186 us -> 53.4 us (0.29)
  the two profiles are of different devices: /device:TPU:0 before, /device:TPU:16 now
where the time goes in v1:
time: 53.4 us; the launch traced here: 53.2 us
  Pallas kernels  50.8 us (95%)
  local copies, waits for them, and re-layouts  2.37 us (4%)
    pallas_call x1, Pallas kernels, local(): pl.pallas_call(functools.partial(kernel, frames, groups, heads), out_shap...  50.8 us
    unnamed x1, local copies, waits for them, and re-layouts  2.37 us

profile of v1, /device:TPU:16, one launch (start us, length us, event | category | flops | bytes accessed | tf_op | source)
XLA Modules:
  0.0 53.2 jit_solution(16831137207623701877)
XLA Ops:
  0.0 50.8 %shard_map.91 = bf16[1,2,256,1152]{3,2,1,0:T(8,128)(2,1)} custom-call(bf16[1,2,256,1152]{3,2,1,0:T(8,128)(2,1)} %latent_hbm.1, bf16[1,2,256,1152]{3,2,1,0:T(8,128)(2,1)} %query_hbm.1, bf16[1,2,256,1152]{3,2,1,0:T(8,128)(2,1)} %key_hbm.1, bf16[1,2,256,1152]{3,2,1,0:T(8,128)(2,1)} %value_hbm.1, bf16[1,2,256,1152]{3,2,1,0:T(8,128)(2,1)} %cached_hbm.1, ...), custom_call_target="tpu_custom_call" | custom-call | flops 12000000000 | bytes 18000000 | tf_op jit(solution)/shard_map/pallas_call | solution.py:352
  50.8 2.4 %copy.11 = bf16[1,2,256,1152]{3,2,1,0:T(8,128)(2,1)} copy(bf16[1,2,256,1152]{3,2,1,0:T(8,128)(2,1)} %shard_map.91) | data formatting | bytes 2359296

commit v2 on v1

--- a/solution.py
+++ b/solution.py
@@ -9,6 +9,7 @@
 from jax.sharding import PartitionSpec as P
 
 EDGE = 64
+PARTS = 2
 LANES = 128
 MESH = pl.DeviceIdType.MESH
 
@@ -26,7 +27,8 @@
     band_ref,
     out_weight_hbm,
     temporal_weight_hbm,
-    mixed_ref,
+    hidden_out,
+    temporal_out,
     query,
     key,
     value,
@@ -40,7 +42,6 @@
     arrived,
     packed,
     attended,
-    returned,
     gather,
     spread,
     load_sem,
@@ -50,15 +51,46 @@
     norm_recv,
     back_send,
     back_recv,
+    hidden_sem,
+    own_sem,
 ):
     _, tiles, rows, width = latent_hbm.shape
     share = rows // frames
+    part = rows // PARTS
+    piece_rows = part // frames
     span = rows + 2 * EDGE
     head_dim = width // heads
     me = lax.axis_index("frames")
     at = lax.axis_index("space")
+    chips = frames // 2
+    chip, core = me // 2, lax.rem(me, 2)
+    steps = [(k, j) for k in range(1, chips) for j in range(2)] + [(0, 1)]
+
+    def target_of(i):
+        k, j = steps[i]
+        return lax.rem(chip + k, chips) * 2 + lax.rem(core + j, 2)
+
+    def source_of(i):
+        k, j = steps[i]
+        return lax.rem(chip + chips - k, chips) * 2 + lax.rem(core + j, 2)
+
+    others = range(frames - 1)
     has_above = at > 0
     has_below = at < groups - 1
+
+    barrier = pltpu.get_barrier_semaphore()
+    for i in others:
+        pl.semaphore_signal(
+            barrier, inc=1, device_id={"frames": target_of(i)}, device_id_type=MESH
+        )
+
+    @pl.when(has_above)
+    def _():
+        pl.semaphore_signal(barrier, inc=1, device_id={"space": at - 1}, device_id_type=MESH)
+
+    @pl.when(has_below)
+    def _():
+        pl.semaphore_signal(barrier, inc=1, device_id={"space": at + 1}, device_id_type=MESH)
 
     loads = []
 
@@ -75,25 +107,6 @@
                 load(src.at[0, t - 1, pl.ds(rows - EDGE, EDGE)], dst.at[t, pl.ds(0, EDGE)])
             if t < tiles - 1:
                 load(src.at[0, t + 1, pl.ds(0, EDGE)], dst.at[t, pl.ds(rows + EDGE, EDGE)])
-    load(cached_hbm.at[0], cached)
-    load(latent_hbm.at[0], latent)
-    load(out_weight_hbm, out_weight)
-    early = len(loads)
-    load(temporal_weight_hbm, temporal_weight)
-
-    barrier = pltpu.get_barrier_semaphore()
-    for d in range(1, frames):
-        pl.semaphore_signal(
-            barrier, inc=1, device_id={"frames": lax.rem(me + d, frames)}, device_id_type=MESH
-        )
-
-    @pl.when(has_above)
-    def _():
-        pl.semaphore_signal(barrier, inc=1, device_id={"space": at - 1}, device_id_type=MESH)
-
-    @pl.when(has_below)
-    def _():
-        pl.semaphore_signal(barrier, inc=1, device_id={"space": at + 1}, device_id_type=MESH)
 
     peers = frames - 1 + jnp.where(has_above, 1, 0) + jnp.where(has_below, 1, 0)
     pl.semaphore_wait(barrier, peers)
@@ -125,6 +138,12 @@
         for i in range(2):
             edge(i, 1, at - 1).start()
 
+    load(cached_hbm.at[0], cached)
+    load(latent_hbm.at[0], latent)
+    load(out_weight_hbm, out_weight)
+    early = len(loads)
+    load(temporal_weight_hbm, temporal_weight)
+
     @pl.when(jnp.logical_not(has_above))
     def _():
         for dst in (key, value):
@@ -164,51 +183,95 @@
     scale = math.log2(math.e) / math.sqrt(head_dim)
     position = lax.broadcasted_iota(jnp.int32, (1, span), 1)
 
-    def norm_copy(t, d):
-        peer = lax.rem(me + d, frames)
+    def norm_copy(t, c, i, peer):
         return pltpu.make_async_remote_copy(
-            src_ref=normed.at[t, peer],
-            dst_ref=arrived.at[t, me],
-            send_sem=norm_send.at[t, d],
-            recv_sem=norm_recv.at[t, d],
+            src_ref=normed.at[t, c, peer],
+            dst_ref=arrived.at[t, me, c],
+            send_sem=norm_send.at[t, c, i],
+            recv_sem=norm_recv.at[t, c, i],
             device_id={"frames": peer},
             device_id_type=MESH,
         )
 
-    def back_copy(t, d):
-        peer = lax.rem(me + d, frames)
+    def norm_in(t, c, i):
+        sender = source_of(i)
+        return pltpu.make_async_remote_copy(
+            src_ref=normed.at[t, c, sender],
+            dst_ref=arrived.at[t, sender, c],
+            send_sem=norm_send.at[t, c, i],
+            recv_sem=norm_recv.at[t, c, i],
+            device_id={"frames": sender},
+            device_id_type=MESH,
+        )
+
+    def back_copy(t, i, peer):
         return pltpu.make_async_remote_copy(
             src_ref=attended.at[t, peer],
-            dst_ref=returned.at[t, me],
-            send_sem=back_send.at[t, d],
-            recv_sem=back_recv.at[t, d],
+            dst_ref=temporal_out.at[0, t, :, me],
+            send_sem=back_send.at[t, i],
+            recv_sem=back_recv.at[t, i],
             device_id={"frames": peer},
             device_id_type=MESH,
         )
 
-    def spatial_tile(t, carry):
+    def back_in(t, i):
+        owner = source_of(i)
+        return pltpu.make_async_remote_copy(
+            src_ref=attended.at[t, owner],
+            dst_ref=temporal_out.at[0, t, :, owner],
+            send_sem=back_send.at[t, i],
+            recv_sem=back_recv.at[t, i],
+            device_id={"frames": owner},
+            device_id_type=MESH,
+        )
+
+    def own_copy(t):
+        return pltpu.make_async_copy(
+            attended.at[t, me], temporal_out.at[0, t, :, me], own_sem.at[t]
+        )
+
+    def hidden_copy(t, c):
+        return pltpu.make_async_copy(
+            hidden.at[t, c], hidden_out.at[0, t, c], hidden_sem.at[t, c]
+        )
+
+    def head_blocks(h):
+        start, stop = h * head_dim, (h + 1) * head_dim
+        return start, stop, start // LANES, -(-stop // LANES)
+
+    def spatial_part(n, carry):
+        t, c = n // PARTS, lax.rem(n, PARTS)
+        here = pl.ds(pl.multiple_of(c * part, part), part)
         whole = at * tiles + t
         low = jnp.where(whole == 0, EDGE, 0)
         high = jnp.where(whole == groups * tiles - 1, rows + EDGE, span)
         bias = jnp.where((position >= low) & (position < high), 0.0, -jnp.inf)
         fresh_here = refreshed_ref[0, t] == 1
-        partial = None
-        for h in range(heads):
-            start, stop = h * head_dim, (h + 1) * head_dim
-            a, b = start // LANES, -(-stop // LANES)
+
+        def scores_of(h):
+            start, stop, a, b = head_blocks(h)
             cols = slice(a * LANES, b * LANES)
             at_col = lax.broadcasted_iota(jnp.int32, (1, (b - a) * LANES), 1) + a * LANES
             mine = (at_col >= start) & (at_col < stop)
-            q = query[t, :, cols] * jnp.where(mine, 1.0, 0.0).astype(jnp.bfloat16)
-            scores = lax.dot_general(
+            q = query[t, here, cols] * jnp.where(mine, 1.0, 0.0).astype(jnp.bfloat16)
+            return lax.dot_general(
                 q, key[t, :, cols], (((1,), (1,)), ((), ())), preferred_element_type=jnp.float32
             )
-            scores = scores + bias
+
+        partial = None
+        ahead = scores_of(0)
+        for h in range(heads):
+            start, stop, a, b = head_blocks(h)
+            scores = ahead + bias
+            if h < heads - 1:
+                ahead = scores_of(h + 1)
             top = jnp.max(scores, axis=-1, keepdims=True)
             expo = jnp.exp2((scores - top) * scale)
             total = jnp.sum(expo, axis=-1, keepdims=True)
             out = jnp.dot(
-                expo.astype(jnp.bfloat16), value[t, :, cols], preferred_element_type=jnp.float32
+                expo.astype(jnp.bfloat16),
+                value[t, :, a * LANES : b * LANES],
+                preferred_element_type=jnp.float32,
             )
             out = out * (1.0 / total)
             for block in range(a, b):
@@ -216,30 +279,32 @@
                 if start > block * LANES:
                     piece = jnp.where(lane + block * LANES >= start, piece, partial)
                 if stop >= (block + 1) * LANES:
-                    old = cached[t, :, block * LANES : (block + 1) * LANES]
+                    old = cached[t, here, block * LANES : (block + 1) * LANES]
                     spatial[:, block * LANES : (block + 1) * LANES] = jnp.where(
                         fresh_here, piece.astype(jnp.bfloat16), old
                     )
                 else:
                     partial = piece
         projected = jnp.dot(spatial[...], out_weight[...], preferred_element_type=jnp.float32)
-        hid = (latent[t].astype(jnp.float32) + projected).astype(jnp.bfloat16)
-        hidden[t] = hid
+        hid = (latent[t, here].astype(jnp.float32) + projected).astype(jnp.bfloat16)
+        hidden[t, c] = hid.reshape(frames, piece_rows, width)
         hid32 = hid.astype(jnp.float32)
         mean = jnp.mean(hid32 * hid32, axis=-1, keepdims=True)
         norm = (hid32 * lax.rsqrt(mean + 1e-06)).astype(jnp.bfloat16)
-        normed[t] = norm.reshape(frames, share, width)
-        for d in range(1, frames):
-            norm_copy(t, frames - d).start()
-        arrived[t, me] = normed[t, me]
+        normed[t, c] = norm.reshape(frames, piece_rows, width)
+        for i in others:
+            norm_copy(t, c, i, target_of(i)).start()
+        hidden_copy(t, c).start()
+        arrived[t, me, c] = normed[t, c, me]
         return carry
 
-    lax.fori_loop(0, tiles, spatial_tile, 0)
+    lax.fori_loop(0, tiles * PARTS, spatial_part, 0)
     loads[early].wait()
 
     def temporal_tile(t, carry):
-        for d in range(1, frames):
-            norm_in(t, d)
+        for c in range(PARTS):
+            for i in others:
+                norm_in(t, c, i).wait_recv()
         block = arrived[t].reshape(frames * share, width)
 
         def project(j, c):
@@ -249,8 +314,8 @@
             return c
 
         lax.fori_loop(0, 3, project, 0)
-        for d in range(1, frames + 1):
-            f = lax.rem(me + frames - d, frames)
+        for i in range(frames):
+            f = target_of(i) if i < frames - 1 else me
             products = packed[0, f][None] * packed[1]
             scores = jnp.dot(
                 products.reshape(frames * share, width),
@@ -272,48 +337,24 @@
             result = wide[0] * packed[2, 0].astype(jnp.float32)
             for g in range(1, frames):
                 result = result + wide[g] * packed[2, g].astype(jnp.float32)
-            result = result.astype(jnp.bfloat16)
-            if d < frames:
-                attended[t, f] = result
-                back_copy(t, frames - d).start()
+            attended[t, f] = result.astype(jnp.bfloat16).reshape(PARTS, piece_rows, width)
+            if i < frames - 1:
+                back_copy(t, i, f).start()
             else:
-                returned[t, me] = result
+                own_copy(t).start()
         return carry
 
-    def norm_in(t, d):
-        sender = lax.rem(me + frames - d, frames)
-        pltpu.make_async_remote_copy(
-            src_ref=normed.at[t, sender],
-            dst_ref=arrived.at[t, sender],
-            send_sem=norm_send.at[t, d],
-            recv_sem=norm_recv.at[t, d],
-            device_id={"frames": sender},
-            device_id_type=MESH,
-        ).wait_recv()
-
     lax.fori_loop(0, tiles, temporal_tile, 0)
 
     for t in range(tiles):
-        for d in range(frames):
-            owner = lax.rem(me + frames - d, frames)
-            if d:
-                pltpu.make_async_remote_copy(
-                    src_ref=attended.at[t, owner],
-                    dst_ref=returned.at[t, owner],
-                    send_sem=back_send.at[t, d],
-                    recv_sem=back_recv.at[t, d],
-                    device_id={"frames": owner},
-                    device_id_type=MESH,
-                ).wait_recv()
-            here = pl.ds(pl.multiple_of(owner * share, share), share)
-            mixed_ref[0, t, here] = (
-                hidden[t, here].astype(jnp.float32) + returned[t, owner].astype(jnp.float32)
-            ).astype(jnp.bfloat16)
-
-    for t in range(tiles):
-        for d in range(1, frames):
-            norm_copy(t, d).wait_send()
-            back_copy(t, d).wait_send()
+        for c in range(PARTS):
+            hidden_copy(t, c).wait()
+            for i in others:
+                norm_copy(t, c, i, target_of(i)).wait_send()
+        own_copy(t).wait()
+        for i in others:
+            back_copy(t, i, target_of(i)).wait_send()
+            back_in(t, i).wait_recv()
 
     @pl.when(has_below)
     def _():
@@ -348,12 +389,13 @@
     anywhere = pl.BlockSpec(memory_space=pl.ANY)
     scalars = pl.BlockSpec(memory_space=pltpu.SMEM)
     dma = pltpu.SemaphoreType.DMA
-    exchanged = pltpu.VMEM((tiles, frames, share, width), bf16)
-    return pl.pallas_call(
+    piece = share // PARTS
+    shape = (1, tiles, PARTS, frames, piece, width)
+    hidden, temporal = pl.pallas_call(
         functools.partial(kernel, frames, groups, heads),
-        out_shape=jax.ShapeDtypeStruct(latent.shape, bf16),
+        out_shape=[jax.ShapeDtypeStruct(shape, bf16)] * 2,
         in_specs=[anywhere] * 5 + [scalars] * 2 + [anywhere] * 2,
-        out_specs=pl.BlockSpec(memory_space=pltpu.VMEM),
+        out_specs=[anywhere] * 2,
         scratch_shapes=[
             pltpu.VMEM((tiles, rows, width), bf16),
             pltpu.VMEM((tiles, span, width), bf16),
@@ -362,22 +404,23 @@
             pltpu.VMEM((tiles, rows, width), bf16),
             pltpu.VMEM(out_weight.shape, bf16),
             pltpu.VMEM(temporal_weight.shape, bf16),
-            pltpu.VMEM((rows, width), bf16),
-            pltpu.VMEM((tiles, rows, width), bf16),
-            exchanged,
-            exchanged,
+            pltpu.VMEM((rows // PARTS, width), bf16),
+            pltpu.VMEM(shape[1:], bf16),
+            pltpu.VMEM(shape[1:], bf16),
+            pltpu.VMEM((tiles, frames, PARTS, piece, width), bf16),
             pltpu.VMEM((3, frames, share, width), bf16),
-            exchanged,
-            exchanged,
+            pltpu.VMEM((tiles, frames, PARTS, piece, width), bf16),
             pltpu.VMEM((width, LANES), bf16),
             pltpu.VMEM((LANES, width), bf16),
             dma((3 * tiles + 4 * (tiles - 1) + 4,)),
             dma((2, 2)),
             dma((2, 2)),
-            dma((tiles, frames)),
-            dma((tiles, frames)),
-            dma((tiles, frames)),
-            dma((tiles, frames)),
+            dma((tiles, PARTS, frames - 1)),
+            dma((tiles, PARTS, frames - 1)),
+            dma((tiles, frames - 1)),
+            dma((tiles, frames - 1)),
+            dma((tiles, PARTS)),
+            dma((tiles,)),
         ],
         compiler_params=pltpu.CompilerParams(
             collective_id=0, has_side_effects=True, vmem_limit_bytes=60 * 1024 * 1024
@@ -396,6 +439,8 @@
         out_weight,
         temporal_weight,
     )
+    mixed = hidden.astype(jnp.float32) + temporal.astype(jnp.float32)
+    return mixed.astype(jnp.bfloat16).reshape(latent.shape)
 
 
 def solution(mesh):

time: 53.4 us -> 54.2 us (1.015)
  the two profiles are of different devices: /device:TPU:16 before, /device:TPU:17 now
where the time goes in v2:
time: 54.2 us; the launch traced here: 54.1 us
  Pallas kernels  51.1 us (94%)
  other arithmetic  2.92 us (5%)
    pallas_call x1, Pallas kernels, local(): pl.pallas_call(functools.partial(kernel, frames, groups, heads), out_shap...  51.1 us
    convert_element_type x1, other arithmetic, local(): return mixed.astype(jnp.bfloat16).reshape(latent.shape)  2.92 us

profile of v2, /device:TPU:17, one launch (start us, length us, event | category | flops | bytes accessed | tf_op | source)
XLA Modules:
  0.0 54.1 jit_solution(6411904800253667860)
XLA Ops:
  0.0 51.1 %shard_map.91 = (bf16[1,2,2,4,32,1152]{5,4,3,2,1,0:T(8,128)(2,1)}, bf16[1,2,2,4,32,1152]{5,4,3,2,1,0:T(8,128)(2,1)}) custom-call(bf16[1,2,256,1152]{3,2,1,0:T(8,128)(2,1)} %latent_hbm.1, bf16[1,2,256,1152]{3,2,1,0:T(8,128)(2,1)} %query_hbm.1, bf16[1,2,256,1152]{3,2,1,0:T(8,128)(2,1)} %key_hbm.1, bf16[1,2,256,1152]{3,2,1,0:T(8,128)(2,1)} %value_hbm.1, ...), custom_call_target="tpu_custom_call" | custom-call | flops 12000000000 | bytes 18000000 | tf_op jit(solution)/shard_map/pallas_call | solution.py:394
  51.2 2.9 %add_convert_fusion = bf16[1,2,2,4,32,1152]{5,4,3,2,1,0:T(8,128)(2,1)} fusion(bf16[1,2,2,4,32,1152]{5,4,3,2,1,0:T(8,128)(2,1)} %get-tuple-element.8, bf16[1,2,2,4,32,1152]{5,4,3,2,1,0:T(8,128)(2,1)} %get-tuple-element.7), kind=kLoop, calls=%fused_computation | loop fusion | flops 2359296 | bytes 3538944 | tf_op jit(solution)/shard_map/convert_element_type | solution.py:443

commit v3 on v2

--- a/solution.py
+++ b/solution.py
@@ -133,11 +133,6 @@
         for i in range(2):
             edge(i, 0, at + 1).start()
 
-    @pl.when(has_above)
-    def _():
-        for i in range(2):
-            edge(i, 1, at - 1).start()
-
     load(cached_hbm.at[0], cached)
     load(latent_hbm.at[0], latent)
     load(out_weight_hbm, out_weight)
@@ -178,7 +173,12 @@
     @pl.when(has_below)
     def _():
         for i in range(2):
-            edge(i, 1, at + 1).wait_recv()
+            edge(i, 0, at + 1).wait_send()
+
+    @pl.when(has_above)
+    def _():
+        for i in range(2):
+            edge(i, 1, at - 1).start()
 
     scale = math.log2(math.e) / math.sqrt(head_dim)
     position = lax.broadcasted_iota(jnp.int32, (1, span), 1)
@@ -241,6 +241,12 @@
 
     def spatial_part(n, carry):
         t, c = n // PARTS, lax.rem(n, PARTS)
+
+        @pl.when(jnp.logical_and(has_below, n == (tiles - 1) * PARTS))
+        def _():
+            for i in range(2):
+                edge(i, 1, at + 1).wait_recv()
+
         here = pl.ds(pl.multiple_of(c * part, part), part)
         whole = at * tiles + t
         low = jnp.where(whole == 0, EDGE, 0)
@@ -356,15 +362,15 @@
             back_copy(t, i, target_of(i)).wait_send()
             back_in(t, i).wait_recv()
 
-    @pl.when(has_below)
-    def _():
-        for i in range(2):
-            edge(i, 0, at + 1).wait_send()
-
     @pl.when(has_above)
     def _():
         for i in range(2):
             edge(i, 1, at - 1).wait_send()
+
+
+def add_kernel(hidden_ref, temporal_ref, mixed_ref):
+    total = hidden_ref[...].astype(jnp.float32) + temporal_ref[...].astype(jnp.float32)
+    mixed_ref[...] = total.astype(jnp.bfloat16)
 
 
 def local(
@@ -439,8 +445,16 @@
         out_weight,
         temporal_weight,
     )
-    mixed = hidden.astype(jnp.float32) + temporal.astype(jnp.float32)
-    return mixed.astype(jnp.bfloat16).reshape(latent.shape)
+    block = pl.BlockSpec((rows // PARTS, width), lambda i: (i, 0))
+    flat = (tiles * rows, width)
+    mixed = pl.pallas_call(
+        add_kernel,
+        out_shape=jax.ShapeDtypeStruct(flat, bf16),
+        grid=(tiles * PARTS,),
+        in_specs=[block, block],
+        out_specs=block,
+    )(hidden.reshape(flat), temporal.reshape(flat))
+    return mixed.reshape(latent.shape)
 
 
 def solution(mesh):

time: 54.2 us -> 48.3 us (0.89)
  the two profiles are of different devices: /device:TPU:17 before, /device:TPU:0 now
where the time goes in v3:
time: 48.3 us; the launch traced here: 47.7 us
  Pallas kernels  47.7 us (99%)
    pallas_call x1, Pallas kernels, local(): pl.pallas_call(functools.partial(kernel, frames, groups, heads), out_shap...  44 us
    pallas_call x1, Pallas kernels, local(): pl.pallas_call(add_kernel, out_shape=jax.ShapeDtypeStruct(flat, bf16), gr...  3.72 us

profile of v3, /device:TPU:0, one launch (start us, length us, event | category | flops | bytes accessed | tf_op | source)
XLA Modules:
  0.0 47.7 jit_solution(12850734816419894886)
XLA Ops:
  0.0 44.0 %shard_map.91 = (bf16[1,2,2,4,32,1152]{5,4,3,2,1,0:T(8,128)(2,1)}, bf16[1,2,2,4,32,1152]{5,4,3,2,1,0:T(8,128)(2,1)}) custom-call(bf16[1,2,256,1152]{3,2,1,0:T(8,128)(2,1)} %latent_hbm.1, bf16[1,2,256,1152]{3,2,1,0:T(8,128)(2,1)} %query_hbm.1, bf16[1,2,256,1152]{3,2,1,0:T(8,128)(2,1)} %key_hbm.1, bf16[1,2,256,1152]{3,2,1,0:T(8,128)(2,1)} %value_hbm.1, ...), custom_call_target="tpu_custom_call" | custom-call | flops 12000000000 | bytes 18000000 | tf_op jit(solution)/shard_map/pallas_call | solution.py:400
  44.0 3.7 %shard_map.92 = bf16[512,1152]{1,0:T(8,128)(2,1)} custom-call(bf16[512,1152]{1,0:T(8,128)(2,1)} %bitcast.3, bf16[512,1152]{1,0:T(8,128)(2,1)} %bitcast.4), custom_call_target="tpu_custom_call" | custom-call | tf_op jit(solution)/shard_map/pallas_call | solution.py:450

commit v4 on v2

--- a/solution.py
+++ b/solution.py
@@ -44,6 +44,9 @@
     attended,
     gather,
     spread,
+    tops,
+    totals,
+    unscaled,
     load_sem,
     edge_send,
     edge_recv,
@@ -58,7 +61,6 @@
     share = rows // frames
     part = rows // PARTS
     piece_rows = part // frames
-    span = rows + 2 * EDGE
     head_dim = width // heads
     me = lax.axis_index("frames")
     at = lax.axis_index("space")
@@ -133,11 +135,7 @@
         for i in range(2):
             edge(i, 0, at + 1).start()
 
-    @pl.when(has_above)
-    def _():
-        for i in range(2):
-            edge(i, 1, at - 1).start()
-
+    ready = len(loads)
     load(cached_hbm.at[0], cached)
     load(latent_hbm.at[0], latent)
     load(out_weight_hbm, out_weight)
@@ -167,21 +165,11 @@
     for h in range(heads):
         band = jnp.where(lane == h, band_ref[h], band)
 
-    for copy in loads[:early]:
+    for copy in loads[:ready]:
         copy.wait()
 
-    @pl.when(has_above)
-    def _():
-        for i in range(2):
-            edge(i, 0, at - 1).wait_recv()
-
-    @pl.when(has_below)
-    def _():
-        for i in range(2):
-            edge(i, 1, at + 1).wait_recv()
 
     scale = math.log2(math.e) / math.sqrt(head_dim)
-    position = lax.broadcasted_iota(jnp.int32, (1, span), 1)
 
     def norm_copy(t, c, i, peer):
         return pltpu.make_async_remote_copy(
@@ -239,43 +227,73 @@
         start, stop = h * head_dim, (h + 1) * head_dim
         return start, stop, start // LANES, -(-stop // LANES)
 
-    def spatial_part(n, carry):
-        t, c = n // PARTS, lax.rem(n, PARTS)
+    def scores_of(h, t, here, keys):
+        start, stop, a, b = head_blocks(h)
+        cols = slice(a * LANES, b * LANES)
+        at_col = lax.broadcasted_iota(jnp.int32, (1, (b - a) * LANES), 1) + a * LANES
+        mine = (at_col >= start) & (at_col < stop)
+        q = query[t, here, cols] * jnp.where(mine, 1.0, 0.0).astype(jnp.bfloat16)
+        return lax.dot_general(
+            q, key[t, keys, cols], (((1,), (1,)), ((), ())), preferred_element_type=jnp.float32
+        )
+
+    def own_keys(t, c):
         here = pl.ds(pl.multiple_of(c * part, part), part)
+        keys = pl.ds(pl.multiple_of(jnp.where(t == 0, EDGE, 0), EDGE), rows + EDGE)
+        partial = None
+        ahead = scores_of(0, t, here, keys)
+        for h in range(heads):
+            start, stop, a, b = head_blocks(h)
+            scores = ahead
+            if h < heads - 1:
+                ahead = scores_of(h + 1, t, here, keys)
+            top = jnp.max(scores, axis=-1, keepdims=True)
+            expo = jnp.exp2((scores - top) * scale)
+            tops[c, h] = top
+            totals[c, h] = jnp.sum(expo, axis=-1, keepdims=True)
+            out = jnp.dot(
+                expo.astype(jnp.bfloat16),
+                value[t, keys, a * LANES : b * LANES],
+                preferred_element_type=jnp.float32,
+            )
+            for block in range(a, b):
+                piece = out[:, (block - a) * LANES : (block - a + 1) * LANES]
+                if start > block * LANES:
+                    piece = jnp.where(lane + block * LANES >= start, piece, partial)
+                if stop >= (block + 1) * LANES:
+                    unscaled[c, :, block * LANES : (block + 1) * LANES] = piece
+                else:
+                    partial = piece
+
+    def edge_keys(t, c):
+        here = pl.ds(pl.multiple_of(c * part, part), part)
+        keys = pl.ds(pl.multiple_of(jnp.where(t == 0, 0, rows + EDGE), EDGE), EDGE)
         whole = at * tiles + t
-        low = jnp.where(whole == 0, EDGE, 0)
-        high = jnp.where(whole == groups * tiles - 1, rows + EDGE, span)
-        bias = jnp.where((position >= low) & (position < high), 0.0, -jnp.inf)
+        absent = (whole == 0) | (whole == groups * tiles - 1)
+        bias = jnp.where(absent, -jnp.inf, 0.0)
         fresh_here = refreshed_ref[0, t] == 1
-
-        def scores_of(h):
-            start, stop, a, b = head_blocks(h)
-            cols = slice(a * LANES, b * LANES)
-            at_col = lax.broadcasted_iota(jnp.int32, (1, (b - a) * LANES), 1) + a * LANES
-            mine = (at_col >= start) & (at_col < stop)
-            q = query[t, here, cols] * jnp.where(mine, 1.0, 0.0).astype(jnp.bfloat16)
-            return lax.dot_general(
-                q, key[t, :, cols], (((1,), (1,)), ((), ())), preferred_element_type=jnp.float32
-            )
-
         partial = None
-        ahead = scores_of(0)
+        ahead = scores_of(0, t, here, keys)
         for h in range(heads):
             start, stop, a, b = head_blocks(h)
             scores = ahead + bias
             if h < heads - 1:
-                ahead = scores_of(h + 1)
-            top = jnp.max(scores, axis=-1, keepdims=True)
+                ahead = scores_of(h + 1, t, here, keys)
+            old_top = tops[c, h]
+            top = jnp.maximum(old_top, jnp.max(scores, axis=-1, keepdims=True))
             expo = jnp.exp2((scores - top) * scale)
-            total = jnp.sum(expo, axis=-1, keepdims=True)
+            shrink = jnp.exp2((old_top - top) * scale)
+            total = totals[c, h] * shrink + jnp.sum(expo, axis=-1, keepdims=True)
             out = jnp.dot(
                 expo.astype(jnp.bfloat16),
-                value[t, :, a * LANES : b * LANES],
+                value[t, keys, a * LANES : b * LANES],
                 preferred_element_type=jnp.float32,
             )
-            out = out * (1.0 / total)
+            inverse = 1.0 / total
             for block in range(a, b):
                 piece = out[:, (block - a) * LANES : (block - a + 1) * LANES]
+                piece = piece + unscaled[c, :, block * LANES : (block + 1) * LANES] * shrink
+                piece = piece * inverse
                 if start > block * LANES:
                     piece = jnp.where(lane + block * LANES >= start, piece, partial)
                 if stop >= (block + 1) * LANES:
@@ -296,9 +314,47 @@
             norm_copy(t, c, i, target_of(i)).start()
         hidden_copy(t, c).start()
         arrived[t, me, c] = normed[t, c, me]
+
+    def spatial_tile(t, carry):
+        def before(c, inner):
+            own_keys(t, c)
+            return inner
+
+        def after(c, inner):
+            edge_keys(t, c)
+            return inner
+
+        lax.fori_loop(0, PARTS, before, 0)
+
+        @pl.when(t == 0)
+        def _():
+            for copy in loads[ready:early]:
+                copy.wait()
+
+        @pl.when(jnp.logical_and(has_above, t == 0))
+        def _():
+            for i in range(2):
+                edge(i, 0, at - 1).wait_recv()
+
+        @pl.when(jnp.logical_and(has_below, t == 0))
+        def _():
+            for i in range(2):
+                edge(i, 0, at + 1).wait_send()
+
+        @pl.when(jnp.logical_and(has_above, t == 0))
+        def _():
+            for i in range(2):
+                edge(i, 1, at - 1).start()
+
+        @pl.when(jnp.logical_and(has_below, t == tiles - 1))
+        def _():
+            for i in range(2):
+                edge(i, 1, at + 1).wait_recv()
+
+        lax.fori_loop(0, PARTS, after, 0)
         return carry
 
-    lax.fori_loop(0, tiles * PARTS, spatial_part, 0)
+    lax.fori_loop(0, tiles, spatial_tile, 0)
     loads[early].wait()
 
     def temporal_tile(t, carry):
@@ -356,11 +412,6 @@
             back_copy(t, i, target_of(i)).wait_send()
             back_in(t, i).wait_recv()
 
-    @pl.when(has_below)
-    def _():
-        for i in range(2):
-            edge(i, 0, at + 1).wait_send()
-
     @pl.when(has_above)
     def _():
         for i in range(2):
@@ -379,7 +430,7 @@
     temporal_weight,
 ):
     frame_count, tiles, rows, width = latent.shape
-    assert frame_count == 1
+    assert frame_count == 1 and tiles == 2
     heads = band_width.shape[0]
     frames = lax.axis_size("frames")
     groups = lax.axis_size("space")
@@ -412,6 +463,9 @@
             pltpu.VMEM((tiles, frames, PARTS, piece, width), bf16),
             pltpu.VMEM((width, LANES), bf16),
             pltpu.VMEM((LANES, width), bf16),
+            pltpu.VMEM((PARTS, heads, rows // PARTS, 1), jnp.float32),
+            pltpu.VMEM((PARTS, heads, rows // PARTS, 1), jnp.float32),
+            pltpu.VMEM((PARTS, rows // PARTS, width), jnp.float32),
             dma((3 * tiles + 4 * (tiles - 1) + 4,)),
             dma((2, 2)),
             dma((2, 2)),

time: 54.2 us -> 53.2 us (0.982)
  the two profiles are of different devices: /device:TPU:17 before, /device:TPU:0 now
where the time goes in v4:
time: 53.2 us; the launch traced here: 52.6 us
  Pallas kernels  49.7 us (93%)
  other arithmetic  2.92 us (5%)
    pallas_call x1, Pallas kernels, local(): pl.pallas_call(functools.partial(kernel, frames, groups, heads), out_shap...  49.7 us
    convert_element_type x1, other arithmetic, local(): return mixed.astype(jnp.bfloat16).reshape(latent.shape)  2.92 us

profile of v4, /device:TPU:0, one launch (start us, length us, event | category | flops | bytes accessed | tf_op | source)
XLA Modules:
  0.0 52.6 jit_solution(17510164954608938733)
XLA Ops:
  0.0 49.7 %shard_map.91 = (bf16[1,2,2,4,32,1152]{5,4,3,2,1,0:T(8,128)(2,1)}, bf16[1,2,2,4,32,1152]{5,4,3,2,1,0:T(8,128)(2,1)}) custom-call(bf16[1,2,256,1152]{3,2,1,0:T(8,128)(2,1)} %latent_hbm.1, bf16[1,2,256,1152]{3,2,1,0:T(8,128)(2,1)} %query_hbm.1, bf16[1,2,256,1152]{3,2,1,0:T(8,128)(2,1)} %key_hbm.1, bf16[1,2,256,1152]{3,2,1,0:T(8,128)(2,1)} %value_hbm.1, ...), custom_call_target="tpu_custom_call" | custom-call | flops 12000000000 | bytes 18000000 | tf_op jit(solution)/shard_map/pallas_call | solution.py:445
  49.7 2.9 %add_convert_fusion = bf16[1,2,2,4,32,1152]{5,4,3,2,1,0:T(8,128)(2,1)} fusion(bf16[1,2,2,4,32,1152]{5,4,3,2,1,0:T(8,128)(2,1)} %get-tuple-element.8, bf16[1,2,2,4,32,1152]{5,4,3,2,1,0:T(8,128)(2,1)} %get-tuple-element.7), kind=kLoop, calls=%fused_computation | loop fusion | flops 2359296 | bytes 3538944 | tf_op jit(solution)/shard_map/convert_element_type | solution.py:497

commit v5 on v3

--- a/solution.py
+++ b/solution.py
@@ -9,7 +9,7 @@
 from jax.sharding import PartitionSpec as P
 
 EDGE = 64
-PARTS = 2
+PARTS = 1
 LANES = 128
 MESH = pl.DeviceIdType.MESH
 
@@ -366,11 +366,6 @@
     def _():
         for i in range(2):
             edge(i, 1, at - 1).wait_send()
-
-
-def add_kernel(hidden_ref, temporal_ref, mixed_ref):
-    total = hidden_ref[...].astype(jnp.float32) + temporal_ref[...].astype(jnp.float32)
-    mixed_ref[...] = total.astype(jnp.bfloat16)
 
 
 def local(
@@ -445,16 +440,8 @@
         out_weight,
         temporal_weight,
     )
-    block = pl.BlockSpec((rows // PARTS, width), lambda i: (i, 0))
-    flat = (tiles * rows, width)
-    mixed = pl.pallas_call(
-        add_kernel,
-        out_shape=jax.ShapeDtypeStruct(flat, bf16),
-        grid=(tiles * PARTS,),
-        in_specs=[block, block],
-        out_specs=block,
-    )(hidden.reshape(flat), temporal.reshape(flat))
-    return mixed.reshape(latent.shape)
+    mixed = hidden.astype(jnp.float32) + temporal.astype(jnp.float32)
+    return mixed.astype(jnp.bfloat16).reshape(latent.shape)
 
 
 def solution(mesh):

time: 48.3 us -> 47.3 us (0.979)
  Pallas kernels: 47.7 us -> 43.8 us
  other arithmetic: 0 us -> 2.93 us
    pallas_call x1 -> x0, Pallas kernels: 3.72 us -> none  [local(): pl.pallas_call(add_kernel, out_shape=jax.ShapeDtypeStruct(flat, bf16), gr...]
    convert_element_type x0 -> x1, other arithmetic: none -> 2.93 us  [local(): return mixed.astype(jnp.bfloat16).reshape(latent.shape)]
where the time goes in v5:
time: 47.3 us; the launch traced here: 46.8 us
  Pallas kernels  43.8 us (93%)
  other arithmetic  2.93 us (6%)
    pallas_call x1, Pallas kernels, local(): pl.pallas_call(functools.partial(kernel, frames, groups, heads), out_shap...  43.8 us
    convert_element_type x1, other arithmetic, local(): return mixed.astype(jnp.bfloat16).reshape(latent.shape)  2.93 us

profile of v5, /device:TPU:0, one launch (start us, length us, event | category | flops | bytes accessed | tf_op | source)
XLA Modules:
  0.0 46.8 jit_solution(4464134973440184137)
XLA Ops:
  0.0 43.8 %shard_map.91 = (bf16[1,2,1,4,64,1152]{5,4,3,2,1,0:T(8,128)(2,1)}, bf16[1,2,1,4,64,1152]{5,4,3,2,1,0:T(8,128)(2,1)}) custom-call(bf16[1,2,256,1152]{3,2,1,0:T(8,128)(2,1)} %latent_hbm.1, bf16[1,2,256,1152]{3,2,1,0:T(8,128)(2,1)} %query_hbm.1, bf16[1,2,256,1152]{3,2,1,0:T(8,128)(2,1)} %key_hbm.1, bf16[1,2,256,1152]{3,2,1,0:T(8,128)(2,1)} %value_hbm.1, ...), custom_call_target="tpu_custom_call" | custom-call | flops 12000000000 | bytes 18000000 | tf_op jit(solution)/shard_map/pallas_call | solution.py:395
  43.8 2.9 %add_convert_fusion = bf16[1,2,1,4,64,1152]{5,4,3,2,1,0:T(8,128)(2,1)} fusion(bf16[1,2,1,4,64,1152]{5,4,3,2,1,0:T(8,128)(2,1)} %get-tuple-element.8, bf16[1,2,1,4,64,1152]{5,4,3,2,1,0:T(8,128)(2,1)} %get-tuple-element.7), kind=kLoop, calls=%fused_computation | loop fusion | flops 2359296 | bytes 3538944 | tf_op jit(solution)/shard_map/convert_element_type | solution.py:444
